TPU v7x, 32 devices: a whole 2x2x4 slice. The times are simulated.
32 devices in a mesh: prow: 16 (over z, y, core), pcol: 2 (over x).
Axes of the slice: x: 2, y: 2, z: 4, core: 2. Of those that a mesh axis runs over, the one named last changes fastest.
Arguments:
- prior_panel: bfloat16 [16384, 12288], P('prow', 'pcol'), may hold values from -0.0546875 to 0.0546875
- prior_solution: bfloat16 [12288, 256], P('pcol', 'prow'), may hold values from -6 to 6
- right_side: bfloat16 [16384, 256], P('prow', 'pcol'), may hold values from -6 to 6
- new_panel: bfloat16 [2, 16384, 512], P(None, 'prow', 'pcol'), may hold values from -0.25 to 0.25
- inverses: bfloat16 [2, 512, 512], P(None, 'pcol'), as said below
Outputs:
- solved: bfloat16 [2, 512, 256], P(None, 'pcol')
- pending: float32 [16384, 256], P('prow', 'pcol')
Inputs may be any that keep to these rules, and one draw needn't show every extreme that they name: `inverses`: each of the two inverse blocks is lower triangular with a positive diagonal.
All inputs are finite; a program needn't handle non-finite values.
Results may differ from a plain program's by a relative error of at most 0.0057.
Values may be sent and summed in bfloat16 or wider, within the bound.
A program may use at most 64 MiB of HBM per device.

v0:
```python
import jax
import jax.numpy as jnp
from jax import lax
from jax.sharding import PartitionSpec as P


def spread(block, axis, owner):
    block = jnp.where(lax.axis_index(axis) == owner, block, jnp.zeros_like(block))
    return lax.psum(block, axis)


def body(prior_panel, prior_solution, right_side, new_panel, inverses):
    local_rows = prior_panel.shape[0]
    block_size = inverses.shape[2]
    pair_rows = 2 * block_size
    partial_value = jnp.dot(
        prior_panel,
        lax.all_gather(prior_solution, "prow", axis=1, tiled=True),
        preferred_element_type=jnp.float32,
    )
    row_ids = lax.axis_index("prow") * local_rows + lax.iota(jnp.int32, local_rows)
    first_panel = jnp.where(
        (row_ids >= block_size)[:, None], new_panel[0], jnp.zeros_like(new_panel[0])
    )
    second_panel = jnp.where(
        (row_ids >= pair_rows)[:, None], new_panel[1], jnp.zeros_like(new_panel[1])
    )
    pending = right_side.astype(jnp.float32) - lax.psum_scatter(
        partial_value, "pcol", scatter_dimension=1, tiled=True
    )
    solved_list = []
    for section, masked in ((0, first_panel), (1, second_panel)):
        diagonal = pending[section * block_size : (section + 1) * block_size].astype(jnp.bfloat16)
        gathered = lax.all_gather(diagonal, "pcol", axis=1, tiled=True)
        result = spread(
            jnp.dot(inverses[section], gathered, preferred_element_type=jnp.float32).astype(
                jnp.bfloat16
            ),
            "prow",
            0,
        )
        update = jnp.dot(masked, result, preferred_element_type=jnp.float32)
        pending = pending - lax.psum_scatter(update, "pcol", scatter_dimension=1, tiled=True)
        solved_list.append(result)
    first_x = solved_list[0]
    second_x = solved_list[1]
    return (jnp.stack([first_x, second_x]), pending)


def solution(mesh):
    return jax.shard_map(
        body,
        mesh=mesh,
        in_specs=(
            P("prow", "pcol"),
            P("pcol", "prow"),
            P("prow", "pcol"),
            P(None, "prow", "pcol"),
            P(None, "pcol", None),
        ),
        out_specs=(P(None, "pcol", None), P("prow", "pcol")),
        check_vma=False,
    )
```

profile of v0, /device:TPU:0, one launch (start us, length us, event | category | flops | bytes accessed | tf_op | source)
XLA Modules:
  0.0 335.1 jit_solution(1964586816087864626)
XLA Ops:
  7.2 0.0 copy-start.1
  7.2 0.0 all-gather.2.cloned.1.call-start
  7.2 0.7 all-gather.2.cloned.1.call-update
  7.9 0.0 copy-start.2
  7.9 0.0 copy-start
  7.9 0.0 reduce-scatter.4.cloned.1.call-start
  8.0 50.2 %all-gather.2.cloned.1.call-done = bf16[6144,256]{0,1:T(8,128)(2,1)} async-done(((bf16[6144,16]{0,1:T(8,128)(2,1)}), bf16[6144,256]{0,1:T(8,128)(2,1)}) %all-gather.2.cloned.1.call-update) | async-done | bytes 3145744 | tf_op jit(solution)/shard_map/all_gather | solution.py:18
  58.2 9.9 %fusion.20 = f32[1024,256]{1,0:T(8,128)} fusion(bf16[1024,6144]{1,0:T(8,128)(2,1)} %param.5, bf16[6144,256]{0,1:T(8,128)(2,1)} %all-gather.2.cloned.1.call-done), kind=kOutput, calls=%fused_computation.29 | convolution fusion | flops 3221225472 | bytes 16777216 | tf_op jit(solution)/shard_map/dot_general | solution.py:16
  68.1 0.0 reduce-scatter.4.cloned.1.call-update
  68.2 0.0 all-reduce.3.cloned.1.call-start
  68.2 19.2 %reduce-scatter.4.cloned.1.call-done = f32[1024,128]{1,0:T(8,128)} async-done(((f32[1024,256]{1,0:T(8,128)}), f32[1024,128]{1,0:T(8,128)}) %reduce-scatter.4.cloned.1.call-update) | async-done | bytes 524304 | tf_op jit(solution)/shard_map/reduce_scatter | solution.py:28
  87.4 0.0 copy-done.1
  87.4 1.1 convert_subtract_fusion
  88.5 5.9 %all_gather.10 = bf16[512,256]{1,0:T(8,128)(2,1)S(1)} all-gather(bf16[512,128]{1,0:T(8,128)(2,1)S(1)} %slice.47), channel_id=1, replica_groups=mesh['prow'=16,'pcol'=2] {'pcol'}, dimensions={1}, use_global_device_ids=true | all-gather | bytes 393216 | tf_op jit(solution)/shard_map/all_gather | solution.py:34
  94.5 0.0 copy-done.2
  94.5 0.9 fusion.1
  95.4 0.0 all-reduce.3.cloned.1.call-update
  95.4 0.0 reduce-scatter.6.cloned.1.call-start
  95.5 87.0 %all-reduce.3.cloned.1.call-done = bf16[256,256]{0,1:T(8,128)(2,1)} async-done(((bf16[256,256]{0,1:T(8,128)(2,1)}), bf16[256,256]{0,1:T(8,128)(2,1)}) %all-reduce.3.cloned.1.call-update) | async-done | bytes 131088 | tf_op jit(solution)/shard_map/psum | solution.py:9
  182.6 0.0 copy-done
  182.6 2.2 fusion.5
  184.8 0.0 reduce-scatter.6.cloned.1.call-update
  184.8 0.0 all-reduce.5.cloned.1.call-start
  184.9 22.0 %reduce-scatter.6.cloned.1.call-done = f32[1024,128]{1,0:T(8,128)} async-done(((f32[1024,256]{1,0:T(8,128)}), f32[1024,128]{1,0:T(8,128)}) %reduce-scatter.6.cloned.1.call-update) | async-done | bytes 524304 | tf_op jit(solution)/shard_map/reduce_scatter | solution.py:43
  206.9 1.1 sub.10
  208.0 6.0 %all_gather.11 = bf16[512,256]{1,0:T(8,128)(2,1)S(1)} all-gather(bf16[512,128]{1,0:T(8,128)(2,1)S(1)} %slice.46), channel_id=1, replica_groups=mesh['prow'=16,'pcol'=2] {'pcol'}, dimensions={1}, use_global_device_ids=true | all-gather | bytes 393216 | tf_op jit(solution)/shard_map/all_gather | solution.py:34
  214.0 0.9 fusion.3
  214.9 0.0 all-reduce.5.cloned.1.call-update
  215.0 0.0 reduce-scatter.8.cloned.1.call-start
  215.0 87.0 %all-reduce.5.cloned.1.call-done = bf16[256,256]{0,1:T(8,128)(2,1)} async-done(((bf16[256,256]{0,1:T(8,128)(2,1)}), bf16[256,256]{0,1:T(8,128)(2,1)}) %all-reduce.5.cloned.1.call-update) | async-done | bytes 131088 | tf_op jit(solution)/shard_map/psum | solution.py:9
  302.0 2.2 fusion.4
  304.3 0.0 reduce-scatter.8.cloned.1.call-update
  304.3 1.0 pad_maximum_fusion
  305.3 0.8 copy.7
  306.1 20.3 %reduce-scatter.8.cloned.1.call-done = f32[1024,128]{1,0:T(8,128)} async-done(((f32[1024,256]{1,0:T(8,128)}), f32[1024,128]{1,0:T(8,128)}) %reduce-scatter.8.cloned.1.call-update) | async-done | bytes 524304 | tf_op jit(solution)/shard_map/reduce_scatter | solution.py:43
  326.4 1.9 sub.11
  (4 shorter events, 0.0 us)
Async XLA Ops:
  7.2 80.3 %copy-start.1 = (bf16[1024,128]{1,0:T(8,128)(2,1)S(1)}, bf16[1024,128]{1,0:T(8,128)(2,1)}, u32[]{:S(2)}) copy-start(bf16[1024,128]{1,0:T(8,128)(2,1)} %param.7) | copy-start | bytes 786436
  7.2 51.0 %all-gather.2.cloned.1.call-start = ((), (), s32[]{:S(2)}) async-start(), calls=%async_computation.3 | async-start | bytes 3342336 | tf_op jit(solution)/shard_map/all_gather | solution.py:18
  7.9 86.6 %copy-start.2 = (bf16[2,256,512]{2,1,0:T(8,128)(2,1)S(1)}, bf16[2,256,512]{2,1,0:T(8,128)(2,1)}, u32[]{:S(2)}) copy-start(bf16[2,256,512]{2,1,0:T(8,128)(2,1)} %param.9) | copy-start | bytes 1572868
  7.9 174.6 %copy-start = (bf16[2,1024,256]{2,1,0:T(8,128)(2,1)S(1)}, bf16[2,1024,256]{2,1,0:T(8,128)(2,1)}, u32[]{:S(2)}) copy-start(bf16[2,1024,256]{2,1,0:T(8,128)(2,1)} %param.8) | copy-start | bytes 3145732
  7.9 79.5 %reduce-scatter.4.cloned.1.call-start = ((), (), s32[]{:S(2)}) async-start(), calls=%async_computation.4 | async-start | bytes 1572864 | tf_op jit(solution)/shard_map/reduce_scatter | solution.py:28
  68.2 114.4 %all-reduce.3.cloned.1.call-start = ((), (), s32[]{:S(2)}) async-start(), calls=%async_computation.5 | async-start | bytes 262144 | tf_op jit(solution)/shard_map/psum | solution.py:9
  95.4 111.5 %reduce-scatter.6.cloned.1.call-start = ((), (), s32[]{:S(2)}) async-start(), calls=%async_computation.6 | async-start | bytes 1572864 | tf_op jit(solution)/shard_map/reduce_scatter | solution.py:43
  184.8 117.2 %all-reduce.5.cloned.1.call-start = ((), (), s32[]{:S(2)}) async-start(), calls=%async_computation.7 | async-start | bytes 262144 | tf_op jit(solution)/shard_map/psum | solution.py:9
  215.0 111.4 %reduce-scatter.8.cloned.1.call-start = ((), (), s32[]{:S(2)}) async-start(), calls=%async_computation.8 | async-start | bytes 1572864 | tf_op jit(solution)/shard_map/reduce_scatter | solution.py:43
Sparse Core Ops, SparseCore 0:
  10.3 47.8 all-gather.1
  68.3 19.1 reduce-scatter.3
  95.6 86.9 all-reduce.2
  184.9 21.9 reduce-scatter.5
  215.1 86.9 all-reduce.4
  304.4 21.9 reduce-scatter.7
where the time goes:
time: 335 us
  waiting for transfers between devices  287 us (86%)
  matrix products  16.2 us (5%)
  between operations  14.2 us (4%)
  blocking collectives  11.9 us (4%)
  other arithmetic  5.08 us (2%)
    psum x2, waiting for transfers between devices, spread(): return lax.psum(block, axis)  174 us
    all_gather x1, waiting for transfers between devices, body(): lax.all_gather(prior_solution, 'prow', axis=1, tiled=True)  50.2 us
    reduce_scatter x2, waiting for transfers between devices, body(): lax.psum_scatter(update, 'pcol', scatter_dimension=1, tiled=True)  42.3 us
    reduce_scatter x1, waiting for transfers between devices, body(): lax.psum_scatter(partial_value, 'pcol', scatter_dimension=1, tiled=True)  19.2 us
    all_gather x2, blocking collectives, body(): gathered = lax.all_gather(diagonal, 'pcol', axis=1, tiled=True)  11.9 us
    dot_general x1, matrix products, body(): jnp.dot(prior_panel, lax.all_gather(prior_solution, 'prow', axis=1, tiled...  9.91 us
  transfers between devices with their start and end apart: 6, of which 6 were waited for; matrix products, arithmetic and copies ran while one was open for 1% of the time, Pallas kernels for 0%

commit v1 on v0

--- a/solution.py
+++ b/solution.py
@@ -2,6 +2,31 @@
 import jax.numpy as jnp
 from jax import lax
 from jax.sharding import PartitionSpec as P
+from jax.lax import axis_index, axis_size, ppermute
+
+
+def enter_patches_in(z, along_dim):
+    local_now = list(z.shape[1:])
+    local_now[along_dim] *= z.shape[0]
+    known = jnp.moveaxis(z, 0, along_dim).reshape(local_now)
+    return known
+
+
+def match_view(xx, where_dim, device_axis):
+    axis_len = axis_size(device_axis)
+    all_rows = list(map(lambda dev_i: (dev_i, (dev_i + 1) % axis_len), range(axis_len)))
+    line_up = [(t, b) for b, t in all_rows]
+    o_now, mid_arr = ([], [])
+    for nth in range(axis_len - 1):
+        if nth % 2 == 0:
+            o_now.append(ppermute(o_now[-1] if o_now else xx, device_axis, all_rows))
+        else:
+            mid_arr.append(ppermute(mid_arr[-1] if mid_arr else xx, device_axis, line_up))
+    u1 = jnp.stack([*o_now[::-1], xx, *mid_arr])
+    raw_out = axis_index(device_axis) - len(o_now)
+    u1 = u1[(jnp.arange(axis_len) - raw_out) % axis_len]
+    mat_out = enter_patches_in(u1, where_dim)
+    return mat_out
 
 
 def spread(block, axis, owner):
@@ -14,9 +39,7 @@
     block_size = inverses.shape[2]
     pair_rows = 2 * block_size
     partial_value = jnp.dot(
-        prior_panel,
-        lax.all_gather(prior_solution, "prow", axis=1, tiled=True),
-        preferred_element_type=jnp.float32,
+        prior_panel, match_view(prior_solution, 1, "prow"), preferred_element_type=jnp.float32
     )
     row_ids = lax.axis_index("prow") * local_rows + lax.iota(jnp.int32, local_rows)
     first_panel = jnp.where(

time: 335 us -> 356 us (1.063)
  starting transfers between devices: 0.24 us -> 33 us
  waiting for transfers between devices: 287 us -> 265 us
  local copies, waits for them, and re-layouts: 0.89 us -> 11.1 us
    all_gather x1 -> x0, waiting for transfers between devices: 50.2 us -> none  [body(): lax.all_gather(prior_solution, 'prow', axis=1, tiled=True)]
    ppermute x0 -> x15, starting transfers between devices: none -> 32.8 us  [the longest x7 32.3 us: match_view(): ppermute(mid_arr[-1] if mid_arr else xx, device_axis, line_up)]
    ppermute x0 -> x15, waiting for transfers between devices: none -> 30.5 us  [the longest x8 27.1 us: match_view(): o_now.append(ppermute(o_now[-1] if o_now else xx, device_axis, all_rows))]
    unnamed x7 -> x60, local copies, waits for them, and re-layouts: 0.85 us -> 8.63 us
  transfers between devices with their start and end apart: 6 -> 20, of which waited for: 6 -> 19; matrix products, arithmetic and copies ran while one was open for 1% -> 2% of each run, Pallas kernels for 0% -> 0%
where the time goes in v1:
time: 356 us; the launch traced here: 355 us
  waiting for transfers between devices  265 us (74%)
  starting transfers between devices  33 us (9%)
  matrix products  16.4 us (5%)
  between operations  14.1 us (4%)
  blocking collectives  11.8 us (3%)
  local copies, waits for them, and re-layouts  11.1 us (3%)
  other arithmetic  4.26 us (1%)
    psum x2, waiting for transfers between devices, spread(): return lax.psum(block, axis)  174 us
    reduce_scatter x2, waiting for transfers between devices, body(): lax.psum_scatter(update, 'pcol', scatter_dimension=1, tiled=True)  42.3 us
    ppermute x7, starting transfers between devices, match_view(): ppermute(mid_arr[-1] if mid_arr else xx, device_axis, line_up)  32.3 us
    ppermute x8, waiting for transfers between devices, match_view(): o_now.append(ppermute(o_now[-1] if o_now else xx, device_axis, all_rows))  27.1 us
    reduce_scatter x1, waiting for transfers between devices, body(): lax.psum_scatter(partial_value, 'pcol', scatter_dimension=1, tiled=True)  17.9 us
    all_gather x2, blocking collectives, body(): gathered = lax.all_gather(diagonal, 'pcol', axis=1, tiled=True)  11.8 us
    dot_general x1, matrix products, body(): jnp.dot(prior_panel, match_view(prior_solution, 1, 'prow'), preferred_ele...  9.98 us
    unnamed x60, local copies, waits for them, and re-layouts  8.63 us
  transfers between devices with their start and end apart: 20, of which 19 were waited for; matrix products, arithmetic and copies ran while one was open for 2% of the time, Pallas kernels for 0%

profile of v1, /device:TPU:0, one launch (start us, length us, event | category | flops | bytes accessed | tf_op | source)
XLA Modules:
  0.0 355.5 jit_solution(15886191368487538575)
XLA Ops:
  7.2 0.0 reduce-scatter.4.cloned.1.call-start
  7.2 0.5 collective-permute-start
  7.7 8.6 %collective-permute-done = bf16[6144,16]{0,1:T(8,128)(2,1)S(1)} collective-permute-done((bf16[6144,16]{0,1:T(8,128)(2,1)}, bf16[6144,16]{0,1:T(8,128)(2,1)S(1)}, u32[]{:S(2)}, u32[]{:S(2)}) %collective-permute-start) | collective-permute-done | bytes 196640 | tf_op jit(solution)/shard_map/ppermute | solution.py:22
  16.3 4.4 %collective-permute-start.8 = (bf16[6144,16]{0,1:T(8,128)(2,1)}, bf16[6144,16]{0,1:T(8,128)(2,1)S(1)}, u32[]{:S(2)}, u32[]{:S(2)}) collective-permute-start(bf16[6144,16]{0,1:T(8,128)(2,1)} %param.6), channel_id=1, source_target_pairs={{2,0},{4,2},{6,4},{8,6},{10,8},{12,10},{14,12},{16,14},{18,16},{20... | collective-permute-start | bytes 589832 | tf_op jit(solution)/shard_map/ppermute | solution.py:24
  20.7 3.3 collective-permute-done.1
  24.1 0.1 collective-permute-done.8
  24.2 0.7 copy-done.4
  24.9 4.6 %collective-permute-start.9 = (bf16[6144,16]{0,1:T(8,128)(2,1)S(1)}, bf16[6144,16]{0,1:T(8,128)(2,1)S(1)}, u32[]{:S(2)}, u32[]{:S(2)}) collective-permute-start(bf16[6144,16]{0,1:T(8,128)(2,1)S(1)} %collective-permute-done.8), channel_id=1, source_target_pairs={{2,0},{4,2},{6,4},{8,6},{10,8},{12,10},{14,12},{16,14},{18,16},{20... | collective-permute-start | bytes 589832 | tf_op jit(solution)/shard_map/ppermute | solution.py:24
  29.5 2.5 collective-permute-done.2
  32.0 0.0 collective-permute-start.3
  32.0 0.7 collective-permute-done.9
  32.7 4.7 %collective-permute-start.10 = (bf16[6144,16]{0,1:T(8,128)(2,1)S(1)}, bf16[6144,16]{0,1:T(8,128)(2,1)S(1)}, u32[]{:S(2)}, u32[]{:S(2)}) collective-permute-start(bf16[6144,16]{0,1:T(8,128)(2,1)S(1)} %collective-permute-done.9), channel_id=1, source_target_pairs={{2,0},{4,2},{6,4},{8,6},{10,8},{12,10},{14,12},{16,14},{18,16},{20... | collective-permute-start | bytes 589832 | tf_op jit(solution)/shard_map/ppermute | solution.py:24
  37.4 2.5 collective-permute-done.3
  39.9 0.0 collective-permute-start.4
  39.9 0.7 collective-permute-done.10
  40.6 4.6 %collective-permute-start.11 = (bf16[6144,16]{0,1:T(8,128)(2,1)S(1)}, bf16[6144,16]{0,1:T(8,128)(2,1)S(1)}, u32[]{:S(2)}, u32[]{:S(2)}) collective-permute-start(bf16[6144,16]{0,1:T(8,128)(2,1)S(1)} %collective-permute-done.10), channel_id=1, source_target_pairs={{2,0},{4,2},{6,4},{8,6},{10,8},{12,10},{14,12},{16,14},{18,16},{20... | collective-permute-start | bytes 589832 | tf_op jit(solution)/shard_map/ppermute | solution.py:24
  45.2 2.6 collective-permute-done.4
  47.8 0.0 collective-permute-start.5
  47.8 0.6 collective-permute-done.11
  48.4 0.1 copy-done.17
  48.5 4.6 %collective-permute-start.12 = (bf16[6144,16]{0,1:T(8,128)(2,1)S(1)}, bf16[6144,16]{0,1:T(8,128)(2,1)S(1)}, u32[]{:S(2)}, u32[]{:S(2)}) collective-permute-start(bf16[6144,16]{0,1:T(8,128)(2,1)S(1)} %collective-permute-done.11), channel_id=1, source_target_pairs={{2,0},{4,2},{6,4},{8,6},{10,8},{12,10},{14,12},{16,14},{18,16},{20... | collective-permute-start | bytes 589832 | tf_op jit(solution)/shard_map/ppermute | solution.py:24
  53.1 2.6 collective-permute-done.5
  55.7 0.0 collective-permute-start.6
  55.7 0.6 collective-permute-done.12
  56.3 4.7 %collective-permute-start.13 = (bf16[6144,16]{0,1:T(8,128)(2,1)S(1)}, bf16[6144,16]{0,1:T(8,128)(2,1)S(1)}, u32[]{:S(2)}, u32[]{:S(2)}) collective-permute-start(bf16[6144,16]{0,1:T(8,128)(2,1)S(1)} %collective-permute-done.12), channel_id=1, source_target_pairs={{2,0},{4,2},{6,4},{8,6},{10,8},{12,10},{14,12},{16,14},{18,16},{20... | collective-permute-start | bytes 589832 | tf_op jit(solution)/shard_map/ppermute | solution.py:24
  61.0 2.6 collective-permute-done.6
  63.6 0.6 collective-permute-done.13
  64.2 4.6 %collective-permute-start.14 = (bf16[6144,16]{0,1:T(8,128)(2,1)S(1)}, bf16[6144,16]{0,1:T(8,128)(2,1)S(1)}, u32[]{:S(2)}, u32[]{:S(2)}) collective-permute-start(bf16[6144,16]{0,1:T(8,128)(2,1)S(1)} %collective-permute-done.13), channel_id=1, source_target_pairs={{2,0},{4,2},{6,4},{8,6},{10,8},{12,10},{14,12},{16,14},{18,16},{20... | collective-permute-start | bytes 589832 | tf_op jit(solution)/shard_map/ppermute | solution.py:24
  68.8 2.5 collective-permute-done.7
  71.4 1.0 bitcast_dynamic-update-slice_fusion.14
  72.4 0.9 bitcast_dynamic-update-slice_fusion.13
  73.3 0.9 bitcast_dynamic-update-slice_fusion.12
  74.3 0.9 bitcast_dynamic-update-slice_fusion.11
  75.2 0.9 bitcast_dynamic-update-slice_fusion.10
  76.2 0.9 bitcast_dynamic-update-slice_fusion.9
  77.4 2.4 gather_fusion
  79.8 10.0 %convolution_bitcast_fusion = f32[1024,256]{0,1:T(8,128)} fusion(bf16[6144,256]{0,1:T(8,128)(2,1)} %bitcast.63, bf16[1024,6144]{1,0:T(8,128)(2,1)} %param.5), kind=kOutput, calls=%fused_computation.1 | convolution fusion | flops 3221225472 | bytes 16777216 | tf_op jit(solution)/shard_map/dot_general | solution.py:41
  89.8 0.0 reduce-scatter.4.cloned.1.call-update
  89.8 0.0 all-reduce.3.cloned.1.call-start
  89.8 0.1 copy.7
  90.0 17.9 %reduce-scatter.4.cloned.1.call-done = f32[1024,128]{0,1:T(8,128)} async-done(((f32[1024,256]{0,1:T(8,128)}), f32[1024,128]{0,1:T(8,128)}) %reduce-scatter.4.cloned.1.call-update) | async-done | bytes 524304 | tf_op jit(solution)/shard_map/reduce_scatter | solution.py:51
  107.9 1.1 convert_subtract_fusion
  109.1 5.9 %all_gather.6 = bf16[512,256]{0,1:T(8,128)(2,1)S(1)} all-gather(bf16[512,128]{0,1:T(8,128)(2,1)S(1)} %slice.49), channel_id=1, replica_groups=mesh['prow'=16,'pcol'=2] {'pcol'}, dimensions={1}, use_global_device_ids=true | all-gather | bytes 393216 | tf_op jit(solution)/shard_map/all_gather | solution.py:57
  115.0 0.9 fusion.1
  115.9 0.0 all-reduce.3.cloned.1.call-update
  115.9 0.0 reduce-scatter.6.cloned.1.call-start
  116.0 87.0 %all-reduce.3.cloned.1.call-done = bf16[256,256]{0,1:T(8,128)(2,1)} async-done(((bf16[256,256]{0,1:T(8,128)(2,1)}), bf16[256,256]{0,1:T(8,128)(2,1)}) %all-reduce.3.cloned.1.call-update) | async-done | bytes 131088 | tf_op jit(solution)/shard_map/psum | solution.py:34
  203.0 2.3 fusion.5
  205.3 0.0 reduce-scatter.6.cloned.1.call-update
  205.3 0.0 all-reduce.5.cloned.1.call-start
  205.4 22.0 %reduce-scatter.6.cloned.1.call-done = f32[1024,128]{0,1:T(8,128)} async-done(((f32[1024,256]{0,1:T(8,128)}), f32[1024,128]{0,1:T(8,128)}) %reduce-scatter.6.cloned.1.call-update) | async-done | bytes 524304 | tf_op jit(solution)/shard_map/reduce_scatter | solution.py:66
  227.4 1.1 sub.29
  228.5 5.9 %all_gather.7 = bf16[512,256]{0,1:T(8,128)(2,1)S(1)} all-gather(bf16[512,128]{0,1:T(8,128)(2,1)S(1)} %slice.48), channel_id=1, replica_groups=mesh['prow'=16,'pcol'=2] {'pcol'}, dimensions={1}, use_global_device_ids=true | all-gather | bytes 393216 | tf_op jit(solution)/shard_map/all_gather | solution.py:57
  234.4 0.9 fusion.3
  235.4 0.0 all-reduce.5.cloned.1.call-update
  235.4 0.0 reduce-scatter.8.cloned.1.call-start
  235.5 87.0 %all-reduce.5.cloned.1.call-done = bf16[256,256]{0,1:T(8,128)(2,1)} async-done(((bf16[256,256]{0,1:T(8,128)(2,1)}), bf16[256,256]{0,1:T(8,128)(2,1)}) %all-reduce.5.cloned.1.call-update) | async-done | bytes 131088 | tf_op jit(solution)/shard_map/psum | solution.py:34
  322.4 2.3 fusion.4
  324.7 0.0 reduce-scatter.8.cloned.1.call-update
  324.8 0.9 pad_maximum_fusion
  325.7 0.8 copy.10
  326.5 20.3 %reduce-scatter.8.cloned.1.call-done = f32[1024,128]{0,1:T(8,128)} async-done(((f32[1024,256]{0,1:T(8,128)}), f32[1024,128]{0,1:T(8,128)}) %reduce-scatter.8.cloned.1.call-update) | async-done | bytes 524304 | tf_op jit(solution)/shard_map/reduce_scatter | solution.py:66
  346.9 1.1 sub.30
  348.0 1.0 copy.11
  (60 shorter events, 0.3 us)
Async XLA Ops:
  7.2 70.0 %copy-start.3 = (bf16[6144,16]{0,1:T(8,128)(2,1)S(1)}, bf16[6144,16]{0,1:T(8,128)(2,1)}, u32[]{:S(2)}) copy-start(bf16[6144,16]{0,1:T(8,128)(2,1)} %param.6) | copy-start | bytes 589828
  7.2 100.8 %reduce-scatter.4.cloned.1.call-start = ((), (), s32[]{:S(2)}) async-start(), calls=%async_computation.3 | async-start | bytes 1572864 | tf_op jit(solution)/shard_map/reduce_scatter | solution.py:51
  7.2 9.1 %collective-permute-start = (bf16[6144,16]{0,1:T(8,128)(2,1)}, bf16[6144,16]{0,1:T(8,128)(2,1)S(1)}, u32[]{:S(2)}, u32[]{:S(2)}) collective-permute-start(bf16[6144,16]{0,1:T(8,128)(2,1)} %param.6), channel_id=1, source_target_pairs={{0,2},{2,4},{4,6},{6,8},{8,10},{10,12},{12,14},{14,16},{16,18},{18... | collective-permute-start | bytes 589832 | tf_op jit(solution)/shard_map/ppermute | solution.py:22
  16.3 7.8 %collective-permute-start.1 = (bf16[6144,16]{0,1:T(8,128)(2,1)S(1)}, bf16[6144,16]{0,1:T(8,128)(2,1)S(1)}, u32[]{:S(2)}, u32[]{:S(2)}) collective-permute-start(bf16[6144,16]{0,1:T(8,128)(2,1)S(1)} %collective-permute-done), channel_id=1, source_target_pairs={{0,2},{2,4},{4,6},{6,8},{8,10},{10,12},{12,14},{14,16},{16,18},{18... | collective-permute-start | bytes 589832 | tf_op jit(solution)/shard_map/ppermute | solution.py:22
  16.3 7.9 %collective-permute-start.8 = (bf16[6144,16]{0,1:T(8,128)(2,1)}, bf16[6144,16]{0,1:T(8,128)(2,1)S(1)}, u32[]{:S(2)}, u32[]{:S(2)}) collective-permute-start(bf16[6144,16]{0,1:T(8,128)(2,1)} %param.6), channel_id=1, source_target_pairs={{2,0},{4,2},{6,4},{8,6},{10,8},{12,10},{14,12},{16,14},{18,16},{20... | collective-permute-start | bytes 589832 | tf_op jit(solution)/shard_map/ppermute | solution.py:24
  24.1 8.6 %copy-start.6 = (bf16[6144,16]{0,1:T(8,128)(2,1)}, bf16[6144,16]{0,1:T(8,128)(2,1)S(1)}, u32[]{:S(2)}) copy-start(bf16[6144,16]{0,1:T(8,128)(2,1)S(1)} %collective-permute-done.1) | copy-start | bytes 589828
  24.1 7.9 %collective-permute-start.2 = (bf16[6144,16]{0,1:T(8,128)(2,1)S(1)}, bf16[6144,16]{0,1:T(8,128)(2,1)S(1)}, u32[]{:S(2)}, u32[]{:S(2)}) collective-permute-start(bf16[6144,16]{0,1:T(8,128)(2,1)S(1)} %collective-permute-done.1), channel_id=1, source_target_pairs={{0,2},{2,4},{4,6},{6,8},{8,10},{10,12},{12,14},{14,16},{16,18},{18... | collective-permute-start | bytes 589832 | tf_op jit(solution)/shard_map/ppermute | solution.py:22
  24.2 0.7 copy-start.4
  24.9 7.8 %collective-permute-start.9 = (bf16[6144,16]{0,1:T(8,128)(2,1)S(1)}, bf16[6144,16]{0,1:T(8,128)(2,1)S(1)}, u32[]{:S(2)}, u32[]{:S(2)}) collective-permute-start(bf16[6144,16]{0,1:T(8,128)(2,1)S(1)} %collective-permute-done.8), channel_id=1, source_target_pairs={{2,0},{4,2},{6,4},{8,6},{10,8},{12,10},{14,12},{16,14},{18,16},{20... | collective-permute-start | bytes 589832 | tf_op jit(solution)/shard_map/ppermute | solution.py:24
  32.0 8.6 %copy-start.9 = (bf16[6144,16]{0,1:T(8,128)(2,1)}, bf16[6144,16]{0,1:T(8,128)(2,1)S(1)}, u32[]{:S(2)}) copy-start(bf16[6144,16]{0,1:T(8,128)(2,1)S(1)} %collective-permute-done.2) | copy-start | bytes 589828
  32.0 7.9 %collective-permute-start.3 = (bf16[6144,16]{0,1:T(8,128)(2,1)S(1)}, bf16[6144,16]{0,1:T(8,128)(2,1)S(1)}, u32[]{:S(2)}, u32[]{:S(2)}) collective-permute-start(bf16[6144,16]{0,1:T(8,128)(2,1)S(1)} %collective-permute-done.2), channel_id=1, source_target_pairs={{0,2},{2,4},{4,6},{6,8},{8,10},{10,12},{12,14},{14,16},{16,18},{18... | collective-permute-start | bytes 589832 | tf_op jit(solution)/shard_map/ppermute | solution.py:22
  32.7 4.7 %copy-start.7 = (bf16[6144,16]{0,1:T(8,128)(2,1)}, bf16[6144,16]{0,1:T(8,128)(2,1)S(1)}, u32[]{:S(2)}) copy-start(bf16[6144,16]{0,1:T(8,128)(2,1)S(1)} %collective-permute-done.9) | copy-start | bytes 589828
  32.7 7.9 %collective-permute-start.10 = (bf16[6144,16]{0,1:T(8,128)(2,1)S(1)}, bf16[6144,16]{0,1:T(8,128)(2,1)S(1)}, u32[]{:S(2)}, u32[]{:S(2)}) collective-permute-start(bf16[6144,16]{0,1:T(8,128)(2,1)S(1)} %collective-permute-done.9), channel_id=1, source_target_pairs={{2,0},{4,2},{6,4},{8,6},{10,8},{12,10},{14,12},{16,14},{18,16},{20... | collective-permute-start | bytes 589832 | tf_op jit(solution)/shard_map/ppermute | solution.py:24
  39.9 28.9 %copy-start.14 = (bf16[6144,16]{0,1:T(8,128)(2,1)}, bf16[6144,16]{0,1:T(8,128)(2,1)S(1)}, u32[]{:S(2)}) copy-start(bf16[6144,16]{0,1:T(8,128)(2,1)S(1)} %collective-permute-done.3) | copy-start | bytes 589828
  39.9 7.9 %collective-permute-start.4 = (bf16[6144,16]{0,1:T(8,128)(2,1)S(1)}, bf16[6144,16]{0,1:T(8,128)(2,1)S(1)}, u32[]{:S(2)}, u32[]{:S(2)}) collective-permute-start(bf16[6144,16]{0,1:T(8,128)(2,1)S(1)} %collective-permute-done.3), channel_id=1, source_target_pairs={{0,2},{2,4},{4,6},{6,8},{8,10},{10,12},{12,14},{14,16},{16,18},{18... | collective-permute-start | bytes 589832 | tf_op jit(solution)/shard_map/ppermute | solution.py:22
  40.6 4.6 %copy-start.10 = (bf16[6144,16]{0,1:T(8,128)(2,1)}, bf16[6144,16]{0,1:T(8,128)(2,1)S(1)}, u32[]{:S(2)}) copy-start(bf16[6144,16]{0,1:T(8,128)(2,1)S(1)} %collective-permute-done.10) | copy-start | bytes 589828
  40.6 7.8 %collective-permute-start.11 = (bf16[6144,16]{0,1:T(8,128)(2,1)S(1)}, bf16[6144,16]{0,1:T(8,128)(2,1)S(1)}, u32[]{:S(2)}, u32[]{:S(2)}) collective-permute-start(bf16[6144,16]{0,1:T(8,128)(2,1)S(1)} %collective-permute-done.10), channel_id=1, source_target_pairs={{2,0},{4,2},{6,4},{8,6},{10,8},{12,10},{14,12},{16,14},{18,16},{20... | collective-permute-start | bytes 589832 | tf_op jit(solution)/shard_map/ppermute | solution.py:24
  47.8 0.7 copy-start.17
  47.8 7.9 %collective-permute-start.5 = (bf16[6144,16]{0,1:T(8,128)(2,1)S(1)}, bf16[6144,16]{0,1:T(8,128)(2,1)S(1)}, u32[]{:S(2)}, u32[]{:S(2)}) collective-permute-start(bf16[6144,16]{0,1:T(8,128)(2,1)S(1)} %collective-permute-done.4), channel_id=1, source_target_pairs={{0,2},{2,4},{4,6},{6,8},{8,10},{10,12},{12,14},{14,16},{16,18},{18... | collective-permute-start | bytes 589832 | tf_op jit(solution)/shard_map/ppermute | solution.py:22
  48.5 20.3 %copy-start.12 = (bf16[6144,16]{0,1:T(8,128)(2,1)}, bf16[6144,16]{0,1:T(8,128)(2,1)S(1)}, u32[]{:S(2)}) copy-start(bf16[6144,16]{0,1:T(8,128)(2,1)S(1)} %collective-permute-done.11) | copy-start | bytes 589828
  48.5 7.8 %collective-permute-start.12 = (bf16[6144,16]{0,1:T(8,128)(2,1)S(1)}, bf16[6144,16]{0,1:T(8,128)(2,1)S(1)}, u32[]{:S(2)}, u32[]{:S(2)}) collective-permute-start(bf16[6144,16]{0,1:T(8,128)(2,1)S(1)} %collective-permute-done.11), channel_id=1, source_target_pairs={{2,0},{4,2},{6,4},{8,6},{10,8},{12,10},{14,12},{16,14},{18,16},{20... | collective-permute-start | bytes 589832 | tf_op jit(solution)/shard_map/ppermute | solution.py:24
  55.7 13.1 %copy-start.18 = (bf16[6144,16]{0,1:T(8,128)(2,1)}, bf16[6144,16]{0,1:T(8,128)(2,1)S(1)}, u32[]{:S(2)}) copy-start(bf16[6144,16]{0,1:T(8,128)(2,1)S(1)} %collective-permute-done.5) | copy-start | bytes 589828
  55.7 7.9 %collective-permute-start.6 = (bf16[6144,16]{0,1:T(8,128)(2,1)S(1)}, bf16[6144,16]{0,1:T(8,128)(2,1)S(1)}, u32[]{:S(2)}, u32[]{:S(2)}) collective-permute-start(bf16[6144,16]{0,1:T(8,128)(2,1)S(1)} %collective-permute-done.5), channel_id=1, source_target_pairs={{0,2},{2,4},{4,6},{6,8},{8,10},{10,12},{12,14},{14,16},{16,18},{18... | collective-permute-start | bytes 589832 | tf_op jit(solution)/shard_map/ppermute | solution.py:22
  55.7 21.5 %copy-start.5 = (bf16[6144,16]{0,1:T(8,128)(2,1)S(1)}, bf16[6144,16]{0,1:T(8,128)(2,1)}, u32[]{:S(2)}) copy-start(bf16[6144,16]{0,1:T(8,128)(2,1)} %copy-done.4) | copy-start | bytes 589828
  55.7 21.5 %copy-start.8 = (bf16[6144,16]{0,1:T(8,128)(2,1)S(1)}, bf16[6144,16]{0,1:T(8,128)(2,1)}, u32[]{:S(2)}) copy-start(bf16[6144,16]{0,1:T(8,128)(2,1)} %copy-done.7) | copy-start | bytes 589828
  55.7 21.5 %copy-start.11 = (bf16[6144,16]{0,1:T(8,128)(2,1)S(1)}, bf16[6144,16]{0,1:T(8,128)(2,1)}, u32[]{:S(2)}) copy-start(bf16[6144,16]{0,1:T(8,128)(2,1)} %copy-done.10) | copy-start | bytes 589828
  56.3 12.5 %copy-start.15 = (bf16[6144,16]{0,1:T(8,128)(2,1)}, bf16[6144,16]{0,1:T(8,128)(2,1)S(1)}, u32[]{:S(2)}) copy-start(bf16[6144,16]{0,1:T(8,128)(2,1)S(1)} %collective-permute-done.12) | copy-start | bytes 589828
  56.3 7.9 %collective-permute-start.13 = (bf16[6144,16]{0,1:T(8,128)(2,1)S(1)}, bf16[6144,16]{0,1:T(8,128)(2,1)S(1)}, u32[]{:S(2)}, u32[]{:S(2)}) collective-permute-start(bf16[6144,16]{0,1:T(8,128)(2,1)S(1)} %collective-permute-done.12), channel_id=1, source_target_pairs={{2,0},{4,2},{6,4},{8,6},{10,8},{12,10},{14,12},{16,14},{18,16},{20... | collective-permute-start | bytes 589832 | tf_op jit(solution)/shard_map/ppermute | solution.py:24
  63.6 5.2 %copy-start.19 = (bf16[6144,16]{0,1:T(8,128)(2,1)}, bf16[6144,16]{0,1:T(8,128)(2,1)S(1)}, u32[]{:S(2)}) copy-start(bf16[6144,16]{0,1:T(8,128)(2,1)S(1)} %collective-permute-done.6) | copy-start | bytes 589828
  63.6 7.8 %collective-permute-start.7 = (bf16[6144,16]{0,1:T(8,128)(2,1)S(1)}, bf16[6144,16]{0,1:T(8,128)(2,1)S(1)}, u32[]{:S(2)}, u32[]{:S(2)}) collective-permute-start(bf16[6144,16]{0,1:T(8,128)(2,1)S(1)} %collective-permute-done.6), channel_id=1, source_target_pairs={{0,2},{2,4},{4,6},{6,8},{8,10},{10,12},{12,14},{14,16},{16,18},{18... | collective-permute-start | bytes 589832 | tf_op jit(solution)/shard_map/ppermute | solution.py:22
  64.2 13.2 %collective-permute-start.14 = (bf16[6144,16]{0,1:T(8,128)(2,1)S(1)}, bf16[6144,16]{0,1:T(8,128)(2,1)S(1)}, u32[]{:S(2)}, u32[]{:S(2)}) collective-permute-start(bf16[6144,16]{0,1:T(8,128)(2,1)S(1)} %collective-permute-done.13), channel_id=1, source_target_pairs={{2,0},{4,2},{6,4},{8,6},{10,8},{12,10},{14,12},{16,14},{18,16},{20... | collective-permute-start | bytes 589832 | tf_op jit(solution)/shard_map/ppermute | solution.py:24
  71.4 5.9 %copy-start.13 = (bf16[6144,16]{0,1:T(8,128)(2,1)S(1)}, bf16[6144,16]{0,1:T(8,128)(2,1)}, u32[]{:S(2)}) copy-start(bf16[6144,16]{0,1:T(8,128)(2,1)} %copy-done.12) | copy-start | bytes 589828
  71.4 5.9 %copy-start.16 = (bf16[6144,16]{0,1:T(8,128)(2,1)S(1)}, bf16[6144,16]{0,1:T(8,128)(2,1)}, u32[]{:S(2)}) copy-start(bf16[6144,16]{0,1:T(8,128)(2,1)} %copy-done.15) | copy-start | bytes 589828
  79.8 10.1 %copy-start.2 = (bf16[1024,128]{1,0:T(8,128)(2,1)S(1)}, bf16[1024,128]{1,0:T(8,128)(2,1)}, u32[]{:S(2)}) copy-start(bf16[1024,128]{1,0:T(8,128)(2,1)} %param.7) | copy-start | bytes 786436
  89.8 25.2 %copy-start.20 = (bf16[2,256,512]{2,1,0:T(8,128)(2,1)S(1)}, bf16[2,256,512]{2,1,0:T(8,128)(2,1)}, u32[]{:S(2)}) copy-start(bf16[2,256,512]{2,1,0:T(8,128)(2,1)} %param.9) | copy-start | bytes 1572868
  89.8 113.2 %copy-start = (bf16[2,1024,256]{2,1,0:T(8,128)(2,1)S(1)}, bf16[2,1024,256]{2,1,0:T(8,128)(2,1)}, u32[]{:S(2)}) copy-start(bf16[2,1024,256]{2,1,0:T(8,128)(2,1)} %param.8) | copy-start | bytes 3145732
  89.8 113.2 %all-reduce.3.cloned.1.call-start = ((), (), s32[]{:S(2)}) async-start(), calls=%async_computation.4 | async-start | bytes 262144 | tf_op jit(solution)/shard_map/psum | solution.py:34
  115.9 111.5 %reduce-scatter.6.cloned.1.call-start = ((), (), s32[]{:S(2)}) async-start(), calls=%async_computation.5 | async-start | bytes 1572864 | tf_op jit(solution)/shard_map/reduce_scatter | solution.py:66
  205.3 119.5 %copy-start.1 = (bf16[256,256]{0,1:T(8,128)(2,1)S(1)}, bf16[256,256]{0,1:T(8,128)(2,1)}, u32[]{:S(2)}) copy-start(bf16[256,256]{0,1:T(8,128)(2,1)} %all-reduce.3.cloned.1.call-done) | copy-start | bytes 393220
  205.3 117.1 %all-reduce.5.cloned.1.call-start = ((), (), s32[]{:S(2)}) async-start(), calls=%async_computation.6 | async-start | bytes 262144 | tf_op jit(solution)/shard_map/psum | solution.py:34
  235.4 111.5 %reduce-scatter.8.cloned.1.call-start = ((), (), s32[]{:S(2)}) async-start(), calls=%async_computation.7 | async-start | bytes 1572864 | tf_op jit(solution)/shard_map/reduce_scatter | solution.py:66
Sparse Core Ops, SparseCore 0:
  89.9 17.9 reduce-scatter.3
  116.1 86.8 all-reduce.2
  205.4 21.9 reduce-scatter.5
  235.5 86.8 all-reduce.4
  324.9 21.9 reduce-scatter.7
